TPU v7x, 32 devices: a whole 2x2x4 slice. The times are simulated.
32 devices in a mesh: group: 2 (over y), term: 4 (over x, core), sector: 4 (over z).
Axes of the slice: x: 2, y: 2, z: 4, core: 2. Of those that a mesh axis runs over, the one named last changes fastest.
Arguments:
- trial: float32 [8, 256, 256], P(('group', 'sector'), 'term'), parts along dimension 0, may hold values from -6 to 6
- precond: float32 [8, 256, 256], P(('group', 'sector'), 'term'), parts along dimension 0, may hold values from 1 to 8
- left_ops: float32 [48, 4, 256, 256], P(('group', 'term'), 'sector'), parts along dimension 0, may hold values from -0.375 to 0.375
- right_ops: float32 [48, 4, 256, 256], P(('group', 'term'), 'sector'), parts along dimension 0, may hold values from -0.375 to 0.375
- links: int32 [48, 4], P(('group', 'term'), 'sector'), parts along dimension 0, may hold values from 0 to 4, as said below
- block_dims: int32 [8, 2], P(('group', 'sector')), parts along dimension 0, may hold values from 128 to 256, as said below
Outputs:
- ground: float32 [8, 256, 256], P(('group', 'sector'), 'term'), parts along dimension 0
- energy: float32 [2], P('group'), parts along dimension 0
There are 2 independent parts, one for each index of `group`. A program takes and returns all parts, laid end to end along the dimension named above; each array names one. Nothing has to cross between parts.
Inputs may be any that keep to these rules, and one draw needn't show every extreme that they name: `links`: 4 marks a term that has no block for that target. `block_dims`: entries beyond these are padding.
All inputs are finite; a program needn't handle non-finite values.
Results may differ from a plain program's by a relative error of at most 0.0003.
Values sent between devices are 32-bit elements; how exact they have to be, the bound alone decides.
A program may use at most 64 MiB of HBM per device.

v0:
```python
import jax
import jax.numpy as jnp
from jax import lax
from jax.sharding import PartitionSpec as P

ITERS = 3


EPS = 1e-06


def collect(vector):
    blocks = lax.all_gather(vector, "sector", axis=0, tiled=True)
    whole = lax.all_gather(blocks, "term", axis=1, tiled=True)
    return whole


def apply_op(vector, left_ops, right_ops, links, mask):
    whole = collect(vector)
    width = whole.shape[2]
    padded = jnp.concatenate([whole, jnp.zeros((1, width, width), jnp.float32)], 0)
    chosen = jnp.take(padded, links, axis=0)
    inner = jnp.einsum("tkab,tkbc->tkac", left_ops, chosen, precision=lax.Precision.HIGHEST)
    partial_value = jnp.einsum("tkac,tkdc->kad", inner, right_ops, precision=lax.Precision.HIGHEST)
    summed = lax.psum_scatter(partial_value, "term", scatter_dimension=1, tiled=True)
    return summed * mask


def on_device(trial, precond, left_ops, right_ops, links, block_dims):
    rows_dev = trial.shape[1]
    width = trial.shape[2]
    count = float(trial.shape[0] * lax.axis_size("sector") * width * width)
    first_row = lax.axis_index("term") * rows_dev
    row_index = first_row + jnp.arange(rows_dev, dtype=jnp.int32)
    col_index = jnp.arange(width, dtype=jnp.int32)
    rows_live = row_index[None, :, None] < block_dims[:, 0][:, None, None]
    cols_live = col_index[None, None, :] < block_dims[:, 1][:, None, None]
    mask = (rows_live & cols_live).astype(jnp.float32)
    vector = trial * mask
    start_norm = lax.psum(jnp.sum(vector * vector), ("term", "sector")) / count
    vector = vector / jnp.sqrt(start_norm + EPS)
    image = apply_op(vector, left_ops, right_ops, links, mask)
    theta = None
    for step in range(ITERS):
        theta = lax.psum(jnp.sum(vector * image), ("term", "sector")) / count
        resid = image - theta * vector
        raw = resid / precond
        along = lax.psum(jnp.sum(vector * raw), ("term", "sector")) / count
        proj = raw - along * vector
        proj_norm = lax.psum(jnp.sum(proj * proj), ("term", "sector")) / count
        basis = proj / jnp.sqrt(proj_norm + EPS)
        himage = apply_op(basis, left_ops, right_ops, links, mask)
        first_cross, second_cross, diag_sum = lax.psum(
            (jnp.sum(vector * himage), jnp.sum(basis * image), jnp.sum(basis * himage)),
            ("term", "sector"),
        )
        cross = 0.5 * (first_cross + second_cross) / count
        diag_c = diag_sum / count
        half = 0.5 * (theta - diag_c)
        spread = jnp.sqrt(half * half + cross * cross)
        lowest = 0.5 * (theta + diag_c) - spread
        coef_x = spread - half
        coef_y = -cross
        length = jnp.sqrt(coef_x * coef_x + coef_y * coef_y)
        vector = (coef_x * vector + coef_y * basis) / length
        image = (coef_x * image + coef_y * himage) / length
        theta = lowest
    return (vector, jnp.reshape(theta, (1,)))


def solution(mesh):
    in_specs = (
        P(("group", "sector"), "term", None),
        P(("group", "sector"), "term", None),
        P(("group", "term"), "sector", None, None),
        P(("group", "term"), "sector", None, None),
        P(("group", "term"), "sector"),
        P(("group", "sector"), None),
    )
    out_specs = (P(("group", "sector"), "term", None), P("group"))
    return jax.shard_map(
        on_device, mesh=mesh, in_specs=in_specs, out_specs=out_specs, check_vma=False
    )
```

profile of v0, /device:TPU:0, one launch (start us, length us, event | category | flops | bytes accessed | tf_op | source)
XLA Modules:
  0.0 717.7 jit_solution(1032198188175581505)
XLA Ops:
  11.4 35.8 %psum.133 = f32[]{:T(128)} all-reduce(f32[]{:T(128)} %multiply_reduce_fusion.18), channel_id=1, replica_groups=mesh['group'=2,'term'=4,'sector'=4] {'term','sector'}, use_global_device_ids=true, to_apply=%region_1.0 | all-reduce | flops 1 | bytes 8 | tf_op jit(solution)/shard_map/psum | solution.py:40
  48.8 14.7 %all_gather.24 = f32[4,64,256]{2,1,0:T(8,128)} all-gather(f32[1,64,256]{2,1,0:T(8,128)S(1)} %fusion.52), channel_id=1, replica_groups=mesh['group'=2,'term'=4,'sector'=4] {'sector'}, dimensions={0}, use_global_device_ids=true | all-gather | bytes 327680 | tf_op jit(solution)/shard_map/all_gather | solution.py:13
  64.9 13.3 %all-gather.5.cloned.1.call-done = f32[4,256,256]{2,1,0:T(8,128)} async-done(((f32[4,64,256]{2,1,0:T(8,128)}), f32[4,256,256]{2,1,0:T(8,128)}) %all-gather.5.cloned.1.call-update) | async-done | bytes 1048592 | tf_op jit(solution)/shard_map/all_gather | solution.py:14
  81.3 3.4 fusion.21
  87.0 20.1 %reduce-scatter.5.cloned.1.call-done = f32[1,64,256]{2,1,0:T(8,128)} async-done(((f32[1,256,256]{2,1,0:T(8,128)}), f32[1,64,256]{2,1,0:T(8,128)}) %reduce-scatter.5.cloned.1.call-update) | async-done | bytes 65552 | tf_op jit(solution)/shard_map/reduce_scatter | solution.py:25
  108.7 33.1 %psum.134 = f32[]{:T(128)} all-reduce(f32[]{:T(128)} %multiply_reduce_fusion.17), channel_id=1, replica_groups=mesh['group'=2,'term'=4,'sector'=4] {'term','sector'}, use_global_device_ids=true, to_apply=%region_4.6 | all-reduce | flops 1 | bytes 8 | tf_op jit(solution)/shard_map/psum | solution.py:45
  144.0 30.3 %psum.135 = f32[]{:T(128)} all-reduce(f32[]{:T(128)} %multiply_reduce_fusion.16), channel_id=1, replica_groups=mesh['group'=2,'term'=4,'sector'=4] {'term','sector'}, use_global_device_ids=true, to_apply=%region_6.8 | all-reduce | flops 1 | bytes 8 | tf_op jit(solution)/shard_map/psum | solution.py:48
  176.4 32.5 %psum.136 = f32[]{:T(128)} all-reduce(f32[]{:T(128)} %multiply_reduce_fusion.15), channel_id=1, replica_groups=mesh['group'=2,'term'=4,'sector'=4] {'term','sector'}, use_global_device_ids=true, to_apply=%region_8.10 | all-reduce | flops 1 | bytes 8 | tf_op jit(solution)/shard_map/psum | solution.py:50
  210.6 15.1 %all_gather.26 = f32[4,64,256]{2,1,0:T(8,128)} all-gather(f32[1,64,256]{2,1,0:T(8,128)S(1)} %broadcast_divide_fusion.2), channel_id=1, replica_groups=mesh['group'=2,'term'=4,'sector'=4] {'sector'}, dimensions={0}, use_global_device_ids=true | all-gather | bytes 327680 | tf_op jit(solution)/shard_map/all_gather | solution.py:13
  225.8 14.5 %all-gather.7.cloned.1.call-done = f32[4,256,256]{2,1,0:T(8,128)} async-done(((f32[4,64,256]{2,1,0:T(8,128)}), f32[4,256,256]{2,1,0:T(8,128)}) %all-gather.7.cloned.1.call-update) | async-done | bytes 1048592 | tf_op jit(solution)/shard_map/all_gather | solution.py:14
  242.7 3.1 gather_fusion.1
  245.8 3.3 fusion.10
  251.3 20.1 %reduce-scatter.7.cloned.1.call-done = f32[1,64,256]{2,1,0:T(8,128)} async-done(((f32[1,256,256]{2,1,0:T(8,128)}), f32[1,64,256]{2,1,0:T(8,128)}) %reduce-scatter.7.cloned.1.call-update) | async-done | bytes 65552 | tf_op jit(solution)/shard_map/reduce_scatter | solution.py:25
  274.4 33.2 %all-reduce.6 = (f32[]{:T(128)}, f32[]{:T(128)}) all-reduce(f32[]{:T(128)} %get-tuple-element.8, f32[]{:T(128)S(6)} %add.128), channel_id=1, replica_groups=mesh['group'=2,'term'=4,'sector'=4] {'term','sector'}, use_global_device_ids=true, to_apply=%region_11.13 | all-reduce | flops 2 | bytes 16 | tf_op jit(solution)/shard_map/psum | solution.py:53
  312.0 30.3 %psum.140 = f32[]{:T(128)} all-reduce(f32[]{:T(128)} %get-tuple-element.21), channel_id=1, replica_groups=mesh['group'=2,'term'=4,'sector'=4] {'term','sector'}, use_global_device_ids=true, to_apply=%region_17.19 | all-reduce | flops 1 | bytes 8 | tf_op jit(solution)/shard_map/psum | solution.py:45
  343.6 32.5 %psum.141 = f32[]{:T(128)} all-reduce(f32[]{:T(128)} %multiply_reduce_fusion.10), channel_id=1, replica_groups=mesh['group'=2,'term'=4,'sector'=4] {'term','sector'}, use_global_device_ids=true, to_apply=%region_19.21 | all-reduce | flops 1 | bytes 8 | tf_op jit(solution)/shard_map/psum | solution.py:48
  377.3 30.3 %psum.142 = f32[]{:T(128)} all-reduce(f32[]{:T(128)} %multiply_reduce_fusion.9), channel_id=1, replica_groups=mesh['group'=2,'term'=4,'sector'=4] {'term','sector'}, use_global_device_ids=true, to_apply=%region_21.23 | all-reduce | flops 1 | bytes 8 | tf_op jit(solution)/shard_map/psum | solution.py:50
  408.4 14.8 %all_gather.28 = f32[4,64,256]{2,1,0:T(8,128)} all-gather(f32[1,64,256]{2,1,0:T(8,128)S(1)} %broadcast_divide_fusion.1), channel_id=1, replica_groups=mesh['group'=2,'term'=4,'sector'=4] {'sector'}, dimensions={0}, use_global_device_ids=true | all-gather | bytes 327680 | tf_op jit(solution)/shard_map/all_gather | solution.py:13
  423.5 16.2 %all-gather.9.cloned.1.call-done = f32[4,256,256]{2,1,0:T(8,128)} async-done(((f32[4,64,256]{2,1,0:T(8,128)}), f32[4,256,256]{2,1,0:T(8,128)}) %all-gather.9.cloned.1.call-update) | async-done | bytes 1048592 | tf_op jit(solution)/shard_map/all_gather | solution.py:14
  442.0 3.1 gather_fusion.2
  445.2 3.3 fusion.6
  450.7 20.1 %reduce-scatter.9.cloned.1.call-done = f32[1,64,256]{2,1,0:T(8,128)} async-done(((f32[1,256,256]{2,1,0:T(8,128)}), f32[1,64,256]{2,1,0:T(8,128)}) %reduce-scatter.9.cloned.1.call-update) | async-done | bytes 65552 | tf_op jit(solution)/shard_map/reduce_scatter | solution.py:25
  473.8 33.1 %all-reduce.5 = (f32[]{:T(128)}, f32[]{:T(128)}) all-reduce(f32[]{:T(128)} %get-tuple-element.6, f32[]{:T(128)S(6)} %add.134), channel_id=1, replica_groups=mesh['group'=2,'term'=4,'sector'=4] {'term','sector'}, use_global_device_ids=true, to_apply=%region_24.26 | all-reduce | flops 2 | bytes 16 | tf_op jit(solution)/shard_map/psum | solution.py:53
  511.2 30.3 %psum.146 = f32[]{:T(128)} all-reduce(f32[]{:T(128)} %get-tuple-element.18), channel_id=1, replica_groups=mesh['group'=2,'term'=4,'sector'=4] {'term','sector'}, use_global_device_ids=true, to_apply=%region_30.32 | all-reduce | flops 1 | bytes 8 | tf_op jit(solution)/shard_map/psum | solution.py:45
  542.8 32.5 %psum.147 = f32[]{:T(128)} all-reduce(f32[]{:T(128)} %multiply_reduce_fusion.4), channel_id=1, replica_groups=mesh['group'=2,'term'=4,'sector'=4] {'term','sector'}, use_global_device_ids=true, to_apply=%region_32.34 | all-reduce | flops 1 | bytes 8 | tf_op jit(solution)/shard_map/psum | solution.py:48
  576.6 30.3 %psum.148 = f32[]{:T(128)} all-reduce(f32[]{:T(128)} %multiply_reduce_fusion.3), channel_id=1, replica_groups=mesh['group'=2,'term'=4,'sector'=4] {'term','sector'}, use_global_device_ids=true, to_apply=%region_34.36 | all-reduce | flops 1 | bytes 8 | tf_op jit(solution)/shard_map/psum | solution.py:50
  607.7 14.8 %all_gather.30 = f32[4,64,256]{2,1,0:T(8,128)} all-gather(f32[1,64,256]{2,1,0:T(8,128)S(1)} %broadcast_divide_fusion), channel_id=1, replica_groups=mesh['group'=2,'term'=4,'sector'=4] {'sector'}, dimensions={0}, use_global_device_ids=true | all-gather | bytes 327680 | tf_op jit(solution)/shard_map/all_gather | solution.py:13
  622.6 16.4 %all-gather.11.cloned.1.call-done = f32[4,256,256]{2,1,0:T(8,128)} async-done(((f32[4,64,256]{2,1,0:T(8,128)}), f32[4,256,256]{2,1,0:T(8,128)}) %all-gather.11.cloned.1.call-update) | async-done | bytes 1048592 | tf_op jit(solution)/shard_map/all_gather | solution.py:14
  641.3 3.1 gather_fusion.3
  644.5 3.3 fusion.2
  649.9 20.2 %reduce-scatter.11.cloned.1.call-done = f32[1,64,256]{2,1,0:T(8,128)} async-done(((f32[1,256,256]{2,1,0:T(8,128)}), f32[1,64,256]{2,1,0:T(8,128)}) %reduce-scatter.11.cloned.1.call-update) | async-done | bytes 65552 | tf_op jit(solution)/shard_map/reduce_scatter | solution.py:25
  673.1 33.2 %all-reduce.4 = (f32[]{:T(128)}, f32[]{:T(128)}) all-reduce(f32[]{:T(128)} %get-tuple-element.4, f32[]{:T(128)S(6)} %add.140), channel_id=1, replica_groups=mesh['group'=2,'term'=4,'sector'=4] {'term','sector'}, use_global_device_ids=true, to_apply=%region_37.39 | all-reduce | flops 2 | bytes 16 | tf_op jit(solution)/shard_map/psum | solution.py:53
  (59 shorter events, 42.9 us)
Async XLA Ops:
  7.2 74.2 %copy-start = (f32[6,1,256,256]{3,2,1,0:T(8,128)S(1)}, f32[6,1,256,256]{3,2,1,0:T(8,128)}, u32[]{:S(2)}) copy-start(f32[6,1,256,256]{3,2,1,0:T(8,128)} %param.10) | copy-start | bytes 4718596
  7.2 71.0 %all-gather.5.cloned.1.call-start = ((), (), s32[]{:S(2)}) async-start(), calls=%async_computation.4 | async-start | bytes 1310720 | tf_op jit(solution)/shard_map/all_gather | solution.py:14
  63.5 43.6 %reduce-scatter.5.cloned.1.call-start = ((), (), s32[]{:S(2)}) async-start(), calls=%async_computation.5 | async-start | bytes 327680 | tf_op jit(solution)/shard_map/reduce_scatter | solution.py:25
  81.3 3.4 copy-start.1
  84.8 22.4 %copy-start.3 = (f32[1,64,256]{2,1,0:T(8,128)S(1)}, f32[1,64,256]{2,1,0:T(8,128)}, u32[]{:S(2)}) copy-start(f32[1,64,256]{2,1,0:T(8,128)} %param.8) | copy-start | bytes 196612
  84.8 57.6 %copy-start.2 = (f32[1,64,256]{2,1,0:T(8,128)S(1)}, f32[1,64,256]{2,1,0:T(8,128)}, u32[]{:S(2)}) copy-start(f32[1,64,256]{2,1,0:T(8,128)} %param.9) | copy-start | bytes 196612
  87.0 153.3 %all-gather.7.cloned.1.call-start = ((), (), s32[]{:S(2)}) async-start(), calls=%async_computation.6 | async-start | bytes 1310720 | tf_op jit(solution)/shard_map/all_gather | solution.py:14
  225.8 45.7 %reduce-scatter.7.cloned.1.call-start = ((), (), s32[]{:S(2)}) async-start(), calls=%async_computation.7 | async-start | bytes 327680 | tf_op jit(solution)/shard_map/reduce_scatter | solution.py:25
  249.1 22.4 %copy-start.4 = (f32[1,64,256]{2,1,0:T(8,128)S(1)}, f32[1,64,256]{2,1,0:T(8,128)}, u32[]{:S(2)}) copy-start(f32[1,64,256]{2,1,0:T(8,128)} %reduce-scatter.5.cloned.1.call-done) | copy-start | bytes 196612
  251.3 188.4 %all-gather.9.cloned.1.call-start = ((), (), s32[]{:S(2)}) async-start(), calls=%async_computation.8 | async-start | bytes 1310720 | tf_op jit(solution)/shard_map/all_gather | solution.py:14
  423.2 47.6 %reduce-scatter.9.cloned.1.call-start = ((), (), s32[]{:S(2)}) async-start(), calls=%async_computation.9 | async-start | bytes 327680 | tf_op jit(solution)/shard_map/reduce_scatter | solution.py:25
  450.6 188.3 %all-gather.11.cloned.1.call-start = ((), (), s32[]{:S(2)}) async-start(), calls=%async_computation.10 | async-start | bytes 1310720 | tf_op jit(solution)/shard_map/all_gather | solution.py:14
  622.5 47.6 %reduce-scatter.11.cloned.1.call-start = ((), (), s32[]{:S(2)}) async-start(), calls=%async_computation.11 | async-start | bytes 327680 | tf_op jit(solution)/shard_map/reduce_scatter | solution.py:25
Sparse Core Ops, SparseCore 0:
  63.6 14.5 all-gather.4
  87.1 20.0 reduce-scatter.4
  225.9 14.3 all-gather.6
  251.4 20.0 reduce-scatter.6
  423.4 16.2 all-gather.8
  450.7 20.0 reduce-scatter.8
  622.6 16.2 all-gather.10
  650.0 20.0 reduce-scatter.10
where the time goes:
time: 719 us; the launch traced here: 718 us
  blocking collectives  477 us (66%)
  waiting for transfers between devices  141 us (20%)
  between operations  34.6 us (5%)
  other arithmetic  21.8 us (3%)
  matrix products  21.8 us (3%)
  local copies, waits for them, and re-layouts  21.1 us (3%)
    psum x3, blocking collectives, on_device(): lax.psum((jnp.sum(vector * himage), jnp.sum(basis * image), jnp.sum(basis...  99.4 us
    psum x3, blocking collectives, on_device(): along = lax.psum(jnp.sum(vector * raw), ('term', 'sector')) / count  95.3 us
    psum x3, blocking collectives, on_device(): theta = lax.psum(jnp.sum(vector * image), ('term', 'sector')) / count  93.6 us
    psum x3, blocking collectives, on_device(): proj_norm = lax.psum(jnp.sum(proj * proj), ('term', 'sector')) / count  93.1 us
    reduce_scatter x4, waiting for transfers between devices, apply_op(): lax.psum_scatter(partial_value, 'term', scatter_dimension=1, tiled=True)  80.6 us
    all_gather x4, waiting for transfers between devices, collect(): whole = lax.all_gather(blocks, 'term', axis=1, tiled=True)  60.3 us
    all_gather x4, blocking collectives, collect(): blocks = lax.all_gather(vector, 'sector', axis=0, tiled=True)  59.5 us
    psum x1, blocking collectives, on_device(): start_norm = lax.psum(jnp.sum(vector * vector), ('term', 'sector')) / count  35.8 us
  transfers between devices with their start and end apart: 8, of which 8 were waited for; matrix products, arithmetic and copies ran while one was open for 0% of the time, Pallas kernels for 0%

commit v1 on v0

v1 whole, which is shorter than its diff:
```python
import functools

import jax
import jax.numpy as jnp
from jax import lax
from jax.experimental import pallas as pl
from jax.experimental.pallas import tpu as pltpu
from jax.sharding import PartitionSpec as P

ITERS = 3
EPS = 1e-06
CORES = 2
CHUNK = 64
MESH = pl.DeviceIdType.MESH
F32 = jnp.float32
BF16 = jnp.bfloat16


def split(value):
    high = value.astype(BF16)
    low = (value - high.astype(F32)).astype(BF16)
    return high, low


def kernel(
    sectors, terms, count,
    links_ref, dims_ref, trial_ref, pre_ref, left_ref, right_ref,
    ground_ref, energy_ref,
    gath, part, rsbuf, vec, img, res, pinv, xcat, lcat, rcat, icat, lraw, rraw,
    ag_send, ag_recv, rs_send, rs_recv, load_sem,
):
    rows, width = trial_ref.shape
    own_terms = lraw.shape[0]
    chips = terms // CORES
    me_t = lax.axis_index("term")
    me_s = lax.axis_index("sector")
    me_x = me_t // CORES
    me_c = lax.rem(me_t, CORES)
    other_c = (CORES - 1) - me_c
    wide = 3 * width
    total_rows = sectors * width
    steps = total_rows // CHUNK
    per_block = width // CHUNK

    def term_at(x, c):
        return x * CORES + c

    def ring(i, d, n):
        return lax.rem(i + d + n, n)

    loads = [
        pltpu.make_async_copy(left_ref, lraw, load_sem.at[0]),
        pltpu.make_async_copy(right_ref, rraw, load_sem.at[1]),
    ]
    for load in loads:
        load.start()

    barrier = pltpu.get_barrier_semaphore()
    for d in range(1, sectors):
        pl.semaphore_signal(
            barrier, inc=1, device_id={"sector": ring(me_s, d, sectors)}, device_id_type=MESH
        )
    for d in range(1, terms):
        pl.semaphore_signal(
            barrier, inc=1, device_id={"term": ring(me_t, d, terms)}, device_id_type=MESH
        )
    pl.semaphore_wait(barrier, sectors + terms - 2)

    def slab(ag, s, t):
        return gath.at[ag, pl.ds(pl.multiple_of(s * width + t * rows, rows), rows)]

    def slab_copy(ag, s, t, to_s, to_t, k):
        here = slab(ag, s, t)
        return pltpu.make_async_remote_copy(
            src_ref=here, dst_ref=here,
            send_sem=ag_send.at[ag, k], recv_sem=ag_recv.at[ag, s * terms + t],
            device_id={"term": to_t, "sector": to_s}, device_id_type=MESH,
        )

    def arrive(ag, s, t):
        slab_copy(ag, s, t, ring(me_s, 1, sectors), me_t, 0).wait_recv()

    k_x = sectors - 1
    k_c = k_x + (chips - 1) * sectors
    n_send = k_c + chips * sectors

    def to_chips(ag, s, d):
        for e in range(1, chips):
            slab_copy(
                ag, s, me_t, me_s, term_at(ring(me_x, e, chips), me_c),
                k_x + (e - 1) * sectors + d,
            ).start()

    def to_core(ag, s, x, d, e):
        slab_copy(
            ag, s, term_at(x, me_c), me_s, term_at(me_x, other_c), k_c + e * sectors + d
        ).start()

    def gather_start(ag):
        for d in range(1, sectors):
            slab_copy(ag, me_s, me_t, ring(me_s, d, sectors), me_t, d - 1).start()
        to_chips(ag, me_s, 0)
        to_core(ag, me_s, me_x, 0, 0)

    def gather_sector(ag):
        for d in range(1, sectors):
            s = ring(me_s, -d, sectors)
            arrive(ag, s, me_t)
            to_chips(ag, s, d)
            to_core(ag, s, me_x, d, 0)

    def gather_chip(ag):
        for e in range(1, chips):
            x = ring(me_x, -e, chips)
            for d in range(sectors):
                s = ring(me_s, -d, sectors)
                arrive(ag, s, term_at(x, me_c))
                to_core(ag, s, x, d, e)

    def gather_core(ag):
        for e in range(chips):
            x = ring(me_x, -e, chips)
            for d in range(sectors):
                arrive(ag, ring(me_s, -d, sectors), term_at(x, other_c))

    def gather_rest(ag):
        gather_sector(ag)
        gather_chip(ag)
        gather_core(ag)

    def fold(value):
        return jnp.sum(value.reshape(CHUNK // 8, 8, width), axis=0)

    def chunk_of(i):
        return pl.ds(pl.multiple_of(i * CHUNK, CHUNK), CHUNK)

    def dots(pick, n):
        def body(i, sums):
            at = chunk_of(i)
            return tuple(a + fold(p) for a, p in zip(sums, pick(at)))

        zero = jnp.zeros((8, width), F32)
        sums = lax.fori_loop(0, steps, body, (zero,) * n, unroll=2)
        out = []
        for a in sums:
            a = jnp.sum(a, axis=0, keepdims=True)
            out.append(jnp.sum(a, axis=1, keepdims=True) / count)
        return out

    def put_x(i, value):
        high, low = split(value)
        block = i // per_block
        off = pl.multiple_of(lax.rem(i, per_block) * CHUNK, CHUNK)
        xcat[block, pl.ds(off, CHUNK), :] = high
        xcat[block, pl.ds(width + off, CHUNK), :] = low
        xcat[block, pl.ds(2 * width + off, CHUNK), :] = high

    def over_chunks(body):
        def step(i, carry):
            body(i, chunk_of(i))
            return carry

        lax.fori_loop(0, steps, step, 0, unroll=2)

    row_index = me_t * rows + lax.broadcasted_iota(jnp.int32, (rows, width), 0)
    col_index = lax.broadcasted_iota(jnp.int32, (rows, width), 1)
    live = (row_index < dims_ref[0]) & (col_index < dims_ref[1])
    mask = jnp.where(live, F32(1), F32(0))
    own = pl.ds(pl.multiple_of(me_s * width + me_t * rows, rows), rows)
    first, pre = ITERS + 1, ITERS + 2
    gath[first, own, :] = trial_ref[...] * mask
    gath[pre, own, :] = pre_ref[...]
    gather_start(first)
    for load in loads:
        load.wait()
    xcat[sectors] = jnp.zeros((wide, width), BF16)

    def prepare(k, carry):
        high, low = split(lraw[k])
        lcat[k, :, 0:width] = high
        lcat[k, :, width : 2 * width] = high
        lcat[k, :, 2 * width :] = low
        high, low = split(rraw[k].T)
        base = pl.multiple_of(k * wide, wide)
        rcat[pl.ds(base, width), :] = high
        rcat[pl.ds(base + width, width), :] = low
        rcat[pl.ds(base + 2 * width, width), :] = high
        return carry

    gather_sector(first)
    lax.fori_loop(0, own_terms, prepare, 0)
    gather_chip(first)
    gather_core(first)
    gather_start(pre)

    (norm,) = dots(lambda at: (gath[first, at, :] * gath[first, at, :],), 1)
    scale = 1.0 / jnp.sqrt(norm + EPS)

    def begin(i, at):
        value = gath[first, at, :] * scale
        vec[at, :] = value
        put_x(i, value)

    over_chunks(begin)

    def rs_copy(it, d):
        to = ring(me_t, d, terms)
        return pltpu.make_async_remote_copy(
            src_ref=part.at[it, pl.ds(pl.multiple_of(to * rows, rows), rows)],
            dst_ref=rsbuf.at[it, d - 1],
            send_sem=rs_send.at[it, d - 1], recv_sem=rs_recv.at[it, d - 1],
            device_id={"term": to}, device_id_type=MESH,
        )

    def multiply(it):
        for k in range(own_terms):
            inner = jnp.dot(lcat[k], xcat[links_ref[k]], preferred_element_type=F32)
            high, low = split(inner)
            icat[:, k * wide : k * wide + width] = high
            icat[:, k * wide + width : k * wide + 2 * width] = high
            icat[:, k * wide + 2 * width : (k + 1) * wide] = low
        part[it] = jnp.dot(icat[...], rcat[...], preferred_element_type=F32)
        for d in range(1, terms):
            rs_copy(it, d).start()

    def collect(it):
        total = part[it, pl.ds(pl.multiple_of(me_t * rows, rows), rows), :]
        for d in range(1, terms):
            rs_copy(it, d).wait_recv()
            total = total + rsbuf[it, d - 1]
        gath[it, own, :] = total * mask
        gather_start(it)

    multiply(0)
    gather_sector(pre)
    collect(0)
    gather_chip(pre)
    gather_core(pre)

    def invert(i, at):
        pinv[at, :] = 1.0 / gath[pre, at, :]

    over_chunks(invert)
    gather_rest(0)
    (theta,) = dots(lambda at: (vec[at, :] * gath[0, at, :],), 1)

    def begin_residual(i, at):
        w = gath[0, at, :]
        img[at, :] = w
        r = (w - theta * vec[at, :]) * pinv[at, :]
        res[at, :] = r
        put_x(i, r)

    over_chunks(begin_residual)

    def iterate(it, theta):
        multiply(it)

        def early(at):
            v, w, r = vec[at, :], img[at, :], res[at, :]
            return v * v, v * w, v * r, r * r, r * w

        vv, vw, along, rr, rw = dots(early, 5)
        collect(it)
        gather_rest(it)

        def late(at):
            h = gath[it, at, :]
            return vec[at, :] * h, res[at, :] * h

        vh, rh = dots(late, 2)
        proj = rr - 2.0 * along * along + along * along * vv
        g = 1.0 / jnp.sqrt(proj + EPS)
        cross = 0.5 * g * ((vh - along * vw) + (rw - along * vw))
        diag_c = g * g * (rh - along * (rw + vh) + along * along * vw)
        half = 0.5 * (theta - diag_c)
        spread = jnp.sqrt(half * half + cross * cross)
        lowest = 0.5 * (theta + diag_c) - spread
        coef_x = spread - half
        coef_y = -cross
        length = jnp.sqrt(coef_x * coef_x + coef_y * coef_y)
        c_new = coef_y * g / length
        c_old = (coef_x - coef_y * g * along) / length

        def update(i, at):
            v = c_old * vec[at, :] + c_new * res[at, :]
            w = c_old * img[at, :] + c_new * gath[it, at, :]
            vec[at, :] = v
            img[at, :] = w
            r = (w - lowest * v) * pinv[at, :]
            res[at, :] = r
            put_x(i, r)

        over_chunks(update)
        return lowest

    theta = lax.fori_loop(1, ITERS + 1, iterate, theta)
    ground_ref[...] = vec[own, :]
    energy_ref[...] = jnp.broadcast_to(theta, energy_ref.shape)

    def finish(ag, carry):
        for k in range(n_send):
            slab_copy(ag, me_s, me_t, ring(me_s, 1, sectors), me_t, k).wait_send()
        return carry

    lax.fori_loop(0, ITERS + 3, finish, 0)

    def finish_rs(it, carry):
        for d in range(1, terms):
            rs_copy(it, d).wait_send()
        return carry

    lax.fori_loop(0, ITERS + 1, finish_rs, 0)


def on_device(trial, precond, left_ops, right_ops, links, block_dims):
    sectors = lax.axis_size("sector")
    terms = lax.axis_size("term")
    _, rows, width = trial.shape
    own_terms = left_ops.shape[0]
    count = float(sectors * width * width)
    applies = ITERS + 1
    gathers = ITERS + 3
    whole = (sectors * width, width)
    vmem = pl.BlockSpec(memory_space=pltpu.VMEM)
    smem = pl.BlockSpec(memory_space=pltpu.SMEM)
    hbm = pl.BlockSpec(memory_space=pl.ANY)
    ground, energy = pl.pallas_call(
        functools.partial(kernel, sectors, terms, count),
        out_shape=(
            jax.ShapeDtypeStruct((rows, width), F32),
            jax.ShapeDtypeStruct((1, 128), F32),
        ),
        in_specs=[smem, smem, vmem, vmem, hbm, hbm],
        out_specs=(vmem, vmem),
        scratch_shapes=[
            pltpu.VMEM((gathers,) + whole, F32),
            pltpu.VMEM((applies, width, width), F32),
            pltpu.VMEM((applies, terms - 1, rows, width), F32),
            pltpu.VMEM(whole, F32),
            pltpu.VMEM(whole, F32),
            pltpu.VMEM(whole, F32),
            pltpu.VMEM(whole, F32),
            pltpu.VMEM((sectors + 1, 3 * width, width), BF16),
            pltpu.VMEM((own_terms, width, 3 * width), BF16),
            pltpu.VMEM((own_terms * 3 * width, width), BF16),
            pltpu.VMEM((width, own_terms * 3 * width), BF16),
            pltpu.VMEM((own_terms, width, width), F32),
            pltpu.VMEM((own_terms, width, width), F32),
            pltpu.SemaphoreType.DMA((gathers, sectors * terms)),
            pltpu.SemaphoreType.DMA((gathers, sectors * terms)),
            pltpu.SemaphoreType.DMA((applies, terms - 1)),
            pltpu.SemaphoreType.DMA((applies, terms - 1)),
            pltpu.SemaphoreType.DMA((2,)),
        ],
        compiler_params=pltpu.CompilerParams(
            collective_id=0, has_side_effects=True, vmem_limit_bytes=52 * 2**20
        ),
    )(
        links.reshape(own_terms),
        block_dims.reshape(2),
        trial.reshape(rows, width),
        precond.reshape(rows, width),
        left_ops.reshape(own_terms, width, width),
        right_ops.reshape(own_terms, width, width),
    )
    return ground.reshape(1, rows, width), energy[0, :1]


def solution(mesh):
    in_specs = (
        P(("group", "sector"), "term", None),
        P(("group", "sector"), "term", None),
        P(("group", "term"), "sector", None, None),
        P(("group", "term"), "sector", None, None),
        P(("group", "term"), "sector"),
        P(("group", "sector"), None),
    )
    out_specs = (P(("group", "sector"), "term", None), P("group"))
    return jax.shard_map(
        on_device, mesh=mesh, in_specs=in_specs, out_specs=out_specs, check_vma=False
    )
```

time: 719 us -> 103 us (0.14)
  blocking collectives: 477 us -> 0 us
  waiting for transfers between devices: 141 us -> 0 us
  Pallas kernels: 0 us -> 95.7 us
  between operations: 34.6 us -> 1.82 us
  matrix products: 21.8 us -> 0 us
  other arithmetic: 21.8 us -> 0 us
  local copies, waits for them, and re-layouts: 21.1 us -> 5.02 us
    psum x13 -> x0, blocking collectives: 417 us -> none  [the longest x3 99.4 us: on_device(): lax.psum((jnp.sum(vector * himage), jnp.sum(basis * image), jnp.sum(basis...]
    pallas_call x0 -> x1, Pallas kernels: none -> 95.7 us  [on_device(): pl.pallas_call(functools.partial(kernel, sectors, terms, count), out_shap...]
    reduce_scatter x4 -> x0, waiting for transfers between devices: 80.6 us -> none  [apply_op(): lax.psum_scatter(partial_value, 'term', scatter_dimension=1, tiled=True)]
    all_gather x4 -> x0, waiting for transfers between devices: 60.3 us -> none  [collect(): whole = lax.all_gather(blocks, 'term', axis=1, tiled=True)]
    all_gather x4 -> x0, blocking collectives: 59.5 us -> none  [collect(): blocks = lax.all_gather(vector, 'sector', axis=0, tiled=True)]
    dot_general x8 -> x0, matrix products: 21.8 us -> none  [the longest x4 13.2 us: apply_op(): jnp.einsum('tkab,tkbc->tkac', left_ops, chosen, precision=lax.Precision.H...]
    reduce_sum x13 -> x0, other arithmetic: 16.6 us -> none  [the longest x3 4.63 us: on_device(): theta = lax.psum(jnp.sum(vector * image), ('term', 'sector')) / count]
    gather x4 -> x0, local copies, waits for them, and re-layouts: 11.1 us -> none  [apply_op(): chosen = jnp.take(padded, links, axis=0)]
  transfers between devices with their start and end apart: 8 -> 0, of which waited for: 8 -> 0; matrix products, arithmetic and copies ran while one was open for 0% -> 0% of each run, Pallas kernels for 0% -> 0%
where the time goes in v1:
time: 103 us
  Pallas kernels  95.7 us (93%)
  local copies, waits for them, and re-layouts  5.02 us (5%)
  between operations  1.82 us (2%)
    pallas_call x1, Pallas kernels, on_device(): pl.pallas_call(functools.partial(kernel, sectors, terms, count), out_shap...  95.7 us
    unnamed x11, local copies, waits for them, and re-layouts  5.02 us

profile of v1, /device:TPU:0, one launch (start us, length us, event | category | flops | bytes accessed | tf_op | source)
XLA Modules:
  0.0 102.5 jit_solution(5883130352451192339)
XLA Ops:
  0.6 0.0 copy-start
  0.6 1.4 %copy-done = f32[6,1,256,256]{3,2,1,0:T(8,128)S(1)} copy-done((f32[6,1,256,256]{3,2,1,0:T(8,128)S(1)}, f32[6,1,256,256]{3,2,1,0:T(8,128)}, u32[]{:S(2)}) %copy-start) | copy-done | bytes 1572888
  2.0 0.0 copy-start.1
  2.0 0.8 copy-done.1
  2.9 0.0 copy-start.2
  2.9 0.8 copy-done.2
  3.7 0.0 copy-start.3
  3.7 0.7 copy-done.3
  4.4 0.0 copy-start.4
  4.4 0.7 copy-done.4
  5.0 95.7 %shard_map.77 = (f32[64,256]{1,0:T(8,128)S(1)}, f32[1,128]{1,0:T(1,128)S(1)}) custom-call(s32[6]{0:T(128)S(1)} %bitcast.13, s32[2]{0:T(128)S(1)} %bitcast.14, f32[64,256]{1,0:T(8,128)S(1)} %bitcast.10, f32[64,256]{1,0:T(8,128)S(1)} %bitcast.11, f32[6,256,256]{2,1,0:T(8,128)S(1)} %bitcast.9, f32[6,256,256]{2,1,0:T(8,128)} %bitcast.16), custom_call_target="tpu_custom_call" | custom-call | tf_op jit(solution)/shard_map/pallas_call | solution.py:328
  100.7 0.6 copy.10
Async XLA Ops:
  0.6 1.4 %copy-start = (f32[6,1,256,256]{3,2,1,0:T(8,128)S(1)}, f32[6,1,256,256]{3,2,1,0:T(8,128)}, u32[]{:S(2)}) copy-start(f32[6,1,256,256]{3,2,1,0:T(8,128)} %param.8) | copy-start | bytes 4718596
  2.0 0.8 copy-start.1
  2.9 0.8 copy-start.2
  3.7 0.7 copy-start.3
  4.4 0.7 copy-start.4

commit v2 on v1

--- a/solution.py
+++ b/solution.py
@@ -26,10 +26,10 @@
     sectors, terms, count,
     links_ref, dims_ref, trial_ref, pre_ref, left_ref, right_ref,
     ground_ref, energy_ref,
-    gath, part, rsbuf, vec, img, res, pinv, xcat, lcat, rcat, icat, lraw, rraw,
-    ag_send, ag_recv, rs_send, rs_recv, load_sem,
+    gath, part, rsbuf, vec, img, res, pinv, xcat, lcat, rcat, icat, lraw, rraw, traw, scal,
+    ag_send, ag_recv, rs_send, rs_recv, sc_send, sc_recv, load_sem,
 ):
-    rows, width = trial_ref.shape
+    rows, width = traw.shape
     own_terms = lraw.shape[0]
     chips = terms // CORES
     me_t = lax.axis_index("term")
@@ -48,23 +48,38 @@
     def ring(i, d, n):
         return lax.rem(i + d + n, n)
 
+    others = [(a, b) for a in range(sectors) for b in range(terms) if a or b]
+    barrier = pltpu.get_barrier_semaphore()
+    for a, b in others:
+        pl.semaphore_signal(
+            barrier, inc=1,
+            device_id={"term": ring(me_t, b, terms), "sector": ring(me_s, a, sectors)},
+            device_id_type=MESH,
+        )
+    first, pre = ITERS, ITERS + 1
+    own = pl.ds(pl.multiple_of(me_s * width + me_t * rows, rows), rows)
+    trial_load = pltpu.make_async_copy(trial_ref, traw, load_sem.at[2])
+    pre_load = pltpu.make_async_copy(pre_ref, gath.at[pre, own], load_sem.at[3])
     loads = [
         pltpu.make_async_copy(left_ref, lraw, load_sem.at[0]),
         pltpu.make_async_copy(right_ref, rraw, load_sem.at[1]),
     ]
+    trial_load.start()
     for load in loads:
         load.start()
-
-    barrier = pltpu.get_barrier_semaphore()
-    for d in range(1, sectors):
-        pl.semaphore_signal(
-            barrier, inc=1, device_id={"sector": ring(me_s, d, sectors)}, device_id_type=MESH
-        )
-    for d in range(1, terms):
-        pl.semaphore_signal(
-            barrier, inc=1, device_id={"term": ring(me_t, d, terms)}, device_id_type=MESH
-        )
-    pl.semaphore_wait(barrier, sectors + terms - 2)
+    pre_load.start()
+
+    if sectors == 4:
+        to_sector = [
+            me_s + 1 - 2 * lax.rem(me_s, 2),
+            lax.rem(me_s + 2, 4),
+            3 - me_s,
+        ]
+        from_sector = to_sector
+    else:
+        to_sector = [ring(me_s, d, sectors) for d in range(1, sectors)]
+        from_sector = [ring(me_s, -d, sectors) for d in range(1, sectors)]
+    sources = [me_s] + from_sector
 
     def slab(ag, s, t):
         return gath.at[ag, pl.ds(pl.multiple_of(s * width + t * rows, rows), rows)]
@@ -98,13 +113,13 @@
 
     def gather_start(ag):
         for d in range(1, sectors):
-            slab_copy(ag, me_s, me_t, ring(me_s, d, sectors), me_t, d - 1).start()
+            slab_copy(ag, me_s, me_t, to_sector[d - 1], me_t, d - 1).start()
         to_chips(ag, me_s, 0)
         to_core(ag, me_s, me_x, 0, 0)
 
     def gather_sector(ag):
         for d in range(1, sectors):
-            s = ring(me_s, -d, sectors)
+            s = sources[d]
             arrive(ag, s, me_t)
             to_chips(ag, s, d)
             to_core(ag, s, me_x, d, 0)
@@ -113,7 +128,7 @@
         for e in range(1, chips):
             x = ring(me_x, -e, chips)
             for d in range(sectors):
-                s = ring(me_s, -d, sectors)
+                s = sources[d]
                 arrive(ag, s, term_at(x, me_c))
                 to_core(ag, s, x, d, e)
 
@@ -121,7 +136,7 @@
         for e in range(chips):
             x = ring(me_x, -e, chips)
             for d in range(sectors):
-                arrive(ag, ring(me_s, -d, sectors), term_at(x, other_c))
+                arrive(ag, sources[d], term_at(x, other_c))
 
     def gather_rest(ag):
         gather_sector(ag)
@@ -166,10 +181,9 @@
     col_index = lax.broadcasted_iota(jnp.int32, (rows, width), 1)
     live = (row_index < dims_ref[0]) & (col_index < dims_ref[1])
     mask = jnp.where(live, F32(1), F32(0))
-    own = pl.ds(pl.multiple_of(me_s * width + me_t * rows, rows), rows)
-    first, pre = ITERS + 1, ITERS + 2
-    gath[first, own, :] = trial_ref[...] * mask
-    gath[pre, own, :] = pre_ref[...]
+    trial_load.wait()
+    gath[first, own, :] = traw[...] * mask
+    pl.semaphore_wait(barrier, len(others))
     gather_start(first)
     for load in loads:
         load.wait()
@@ -191,6 +205,7 @@
     lax.fori_loop(0, own_terms, prepare, 0)
     gather_chip(first)
     gather_core(first)
+    pre_load.wait()
     gather_start(pre)
 
     (norm,) = dots(lambda at: (gath[first, at, :] * gath[first, at, :],), 1)
@@ -220,6 +235,8 @@
             icat[:, k * wide + width : k * wide + 2 * width] = high
             icat[:, k * wide + 2 * width : (k + 1) * wide] = low
         part[it] = jnp.dot(icat[...], rcat[...], preferred_element_type=F32)
+
+    def rs_start(it):
         for d in range(1, terms):
             rs_copy(it, d).start()
 
@@ -232,6 +249,7 @@
         gather_start(it)
 
     multiply(0)
+    rs_start(0)
     gather_sector(pre)
     collect(0)
     gather_chip(pre)
@@ -253,22 +271,11 @@
 
     over_chunks(begin_residual)
 
-    def iterate(it, theta):
-        multiply(it)
-
-        def early(at):
-            v, w, r = vec[at, :], img[at, :], res[at, :]
-            return v * v, v * w, v * r, r * r, r * w
-
-        vv, vw, along, rr, rw = dots(early, 5)
-        collect(it)
-        gather_rest(it)
-
-        def late(at):
-            h = gath[it, at, :]
-            return vec[at, :] * h, res[at, :] * h
-
-        vh, rh = dots(late, 2)
+    def early(at):
+        v, w, r = vec[at, :], img[at, :], res[at, :]
+        return v * v, v * w, v * r, r * r, r * w
+
+    def rotate(theta, vv, vw, along, rr, rw, vh, rh):
         proj = rr - 2.0 * along * along + along * along * vv
         g = 1.0 / jnp.sqrt(proj + EPS)
         cross = 0.5 * g * ((vh - along * vw) + (rw - along * vw))
@@ -281,6 +288,21 @@
         length = jnp.sqrt(coef_x * coef_x + coef_y * coef_y)
         c_new = coef_y * g / length
         c_old = (coef_x - coef_y * g * along) / length
+        return lowest, c_old, c_new
+
+    def iterate(it, theta):
+        multiply(it)
+        rs_start(it)
+        known = dots(early, 5)
+        collect(it)
+        gather_rest(it)
+
+        def late(at):
+            h = gath[it, at, :]
+            return vec[at, :] * h, res[at, :] * h
+
+        vh, rh = dots(late, 2)
+        lowest, c_old, c_new = rotate(theta, *known, vh, rh)
 
         def update(i, at):
             v = c_old * vec[at, :] + c_new * res[at, :]
@@ -294,8 +316,46 @@
         over_chunks(update)
         return lowest
 
-    theta = lax.fori_loop(1, ITERS + 1, iterate, theta)
-    ground_ref[...] = vec[own, :]
+    theta = lax.fori_loop(1, ITERS, iterate, theta)
+
+    multiply(ITERS)
+    me = me_s * terms + me_t
+
+    def sc_copy(k):
+        a, b = others[k]
+        return pltpu.make_async_remote_copy(
+            src_ref=scal.at[me], dst_ref=scal.at[me],
+            send_sem=sc_send.at[k], recv_sem=sc_recv.at[me],
+            device_id={"term": ring(me_t, b, terms), "sector": ring(me_s, a, sectors)},
+            device_id_type=MESH,
+        )
+
+    vh, rh = jnp.zeros((8, width), F32), jnp.zeros((8, width), F32)
+    for i in range(per_block):
+        at = pl.ds(pl.multiple_of(me_s * width + i * CHUNK, CHUNK), CHUNK)
+        h = part[ITERS, i * CHUNK : (i + 1) * CHUNK, :]
+        vh = vh + fold(vec[at, :] * h)
+        rh = rh + fold(res[at, :] * h)
+    scal[me, 0:8, :] = vh
+    scal[me, 8:16, :] = rh
+    for k in range(len(others)):
+        sc_copy(k).start()
+    known = dots(early, 5)
+    for a, b in others:
+        source = ring(me_s, a, sectors) * terms + ring(me_t, b, terms)
+        pltpu.make_async_remote_copy(
+            src_ref=scal.at[source], dst_ref=scal.at[source],
+            send_sem=sc_send.at[0], recv_sem=sc_recv.at[source],
+            device_id={"sector": ring(me_s, 1, sectors)}, device_id_type=MESH,
+        ).wait_recv()
+    sums = jnp.sum(scal[...], axis=0)
+
+    def whole_sum(value):
+        value = jnp.sum(value, axis=0, keepdims=True)
+        return jnp.sum(value, axis=1, keepdims=True) / count
+
+    theta, c_old, c_new = rotate(theta, *known, whole_sum(sums[0:8]), whole_sum(sums[8:16]))
+    ground_ref[...] = c_old * vec[own, :] + c_new * res[own, :]
     energy_ref[...] = jnp.broadcast_to(theta, energy_ref.shape)
 
     def finish(ag, carry):
@@ -303,14 +363,16 @@
             slab_copy(ag, me_s, me_t, ring(me_s, 1, sectors), me_t, k).wait_send()
         return carry
 
-    lax.fori_loop(0, ITERS + 3, finish, 0)
+    lax.fori_loop(0, ITERS + 2, finish, 0)
 
     def finish_rs(it, carry):
         for d in range(1, terms):
             rs_copy(it, d).wait_send()
         return carry
 
-    lax.fori_loop(0, ITERS + 1, finish_rs, 0)
+    lax.fori_loop(0, ITERS, finish_rs, 0)
+    for k in range(len(others)):
+        sc_copy(k).wait_send()
 
 
 def on_device(trial, precond, left_ops, right_ops, links, block_dims):
@@ -320,23 +382,23 @@
     own_terms = left_ops.shape[0]
     count = float(sectors * width * width)
     applies = ITERS + 1
-    gathers = ITERS + 3
+    gathers = ITERS + 2
     whole = (sectors * width, width)
     vmem = pl.BlockSpec(memory_space=pltpu.VMEM)
     smem = pl.BlockSpec(memory_space=pltpu.SMEM)
-    hbm = pl.BlockSpec(memory_space=pl.ANY)
+    hbm = pl.BlockSpec(memory_space=pltpu.HBM)
     ground, energy = pl.pallas_call(
         functools.partial(kernel, sectors, terms, count),
         out_shape=(
             jax.ShapeDtypeStruct((rows, width), F32),
             jax.ShapeDtypeStruct((1, 128), F32),
         ),
-        in_specs=[smem, smem, vmem, vmem, hbm, hbm],
+        in_specs=[smem, smem, hbm, hbm, hbm, hbm],
         out_specs=(vmem, vmem),
         scratch_shapes=[
             pltpu.VMEM((gathers,) + whole, F32),
             pltpu.VMEM((applies, width, width), F32),
-            pltpu.VMEM((applies, terms - 1, rows, width), F32),
+            pltpu.VMEM((ITERS, terms - 1, rows, width), F32),
             pltpu.VMEM(whole, F32),
             pltpu.VMEM(whole, F32),
             pltpu.VMEM(whole, F32),
@@ -347,11 +409,15 @@
             pltpu.VMEM((width, own_terms * 3 * width), BF16),
             pltpu.VMEM((own_terms, width, width), F32),
             pltpu.VMEM((own_terms, width, width), F32),
+            pltpu.VMEM((rows, width), F32),
+            pltpu.VMEM((sectors * terms, 16, width), F32),
             pltpu.SemaphoreType.DMA((gathers, sectors * terms)),
             pltpu.SemaphoreType.DMA((gathers, sectors * terms)),
-            pltpu.SemaphoreType.DMA((applies, terms - 1)),
-            pltpu.SemaphoreType.DMA((applies, terms - 1)),
-            pltpu.SemaphoreType.DMA((2,)),
+            pltpu.SemaphoreType.DMA((ITERS, terms - 1)),
+            pltpu.SemaphoreType.DMA((ITERS, terms - 1)),
+            pltpu.SemaphoreType.DMA((sectors * terms,)),
+            pltpu.SemaphoreType.DMA((sectors * terms,)),
+            pltpu.SemaphoreType.DMA((4,)),
         ],
         compiler_params=pltpu.CompilerParams(
             collective_id=0, has_side_effects=True, vmem_limit_bytes=52 * 2**20

time: 103 us -> 92.5 us (0.90)
  Pallas kernels: 95.7 us -> 85.4 us
    pallas_call x1, Pallas kernels: 95.7 us -> 85.4 us  [on_device(): pl.pallas_call(functools.partial(kernel, sectors, terms, count), out_shap...]
where the time goes in v2:
time: 92.5 us; the launch traced here: 92.2 us
  Pallas kernels  85.4 us (92%)
  local copies, waits for them, and re-layouts  5.02 us (5%)
  between operations  1.82 us (2%)
    pallas_call x1, Pallas kernels, on_device(): pl.pallas_call(functools.partial(kernel, sectors, terms, count), out_shap...  85.4 us
    unnamed x11, local copies, waits for them, and re-layouts  5.02 us

profile of v2, /device:TPU:0, one launch (start us, length us, event | category | flops | bytes accessed | tf_op | source)
XLA Modules:
  0.0 92.2 jit_solution(9911228966306711179)
XLA Ops:
  0.6 0.0 copy-start
  0.6 1.4 %copy-done = f32[6,1,256,256]{3,2,1,0:T(8,128)S(1)} copy-done((f32[6,1,256,256]{3,2,1,0:T(8,128)S(1)}, f32[6,1,256,256]{3,2,1,0:T(8,128)}, u32[]{:S(2)}) %copy-start) | copy-done | bytes 1572888
  2.0 0.0 copy-start.1
  2.0 0.8 copy-done.1
  2.9 0.0 copy-start.2
  2.9 0.8 copy-done.2
  3.7 0.0 copy-start.3
  3.7 0.7 copy-done.3
  4.4 0.0 copy-start.4
  4.4 0.7 copy-done.4
  5.0 85.4 %shard_map.77 = (f32[64,256]{1,0:T(8,128)S(1)}, f32[1,128]{1,0:T(1,128)S(1)}) custom-call(s32[6]{0:T(128)S(1)} %bitcast.13, s32[2]{0:T(128)S(1)} %bitcast.14, f32[64,256]{1,0:T(8,128)S(1)} %bitcast.10, f32[64,256]{1,0:T(8,128)S(1)} %bitcast.11, f32[6,256,256]{2,1,0:T(8,128)S(1)} %bitcast.9, f32[6,256,256]{2,1,0:T(8,128)} %bitcast.16), custom_call_target="tpu_custom_call" | custom-call | tf_op jit(solution)/shard_map/pallas_call | solution.py:390
  90.4 0.6 copy.10
Async XLA Ops:
  0.6 1.4 %copy-start = (f32[6,1,256,256]{3,2,1,0:T(8,128)S(1)}, f32[6,1,256,256]{3,2,1,0:T(8,128)}, u32[]{:S(2)}) copy-start(f32[6,1,256,256]{3,2,1,0:T(8,128)} %param.8) | copy-start | bytes 4718596
  2.0 0.8 copy-start.1
  2.9 0.8 copy-start.2
  3.7 0.7 copy-start.3
  4.4 0.7 copy-start.4

commit v3 on v2

--- a/solution.py
+++ b/solution.py
@@ -11,6 +11,7 @@
 EPS = 1e-06
 CORES = 2
 CHUNK = 64
+PARTS = 1
 MESH = pl.DeviceIdType.MESH
 F32 = jnp.float32
 BF16 = jnp.bfloat16
@@ -24,9 +25,9 @@
 
 def kernel(
     sectors, terms, count,
-    links_ref, dims_ref, trial_ref, pre_ref, left_ref, right_ref,
+    links_hbm, dims_hbm, trial_ref, pre_ref, left_ref, right_ref,
     ground_ref, energy_ref,
-    gath, part, rsbuf, vec, img, res, pinv, xcat, lcat, rcat, icat, lraw, rraw, traw, scal,
+    gath, part, rsbuf, vec, img, res, pinv, xcat, lcat, rcat, icat, lraw, rraw, traw, scal, links_ref, dims_ref,
     ag_send, ag_recv, rs_send, rs_recv, sc_send, sc_recv, load_sem,
 ):
     rows, width = traw.shape
@@ -38,6 +39,9 @@
     me_c = lax.rem(me_t, CORES)
     other_c = (CORES - 1) - me_c
     wide = 3 * width
+    quad = sectors == 4 and terms == 2 * CORES
+    parts = PARTS if quad else 1
+    piece = rows // parts
     total_rows = sectors * width
     steps = total_rows // CHUNK
     per_block = width // CHUNK
@@ -64,84 +68,114 @@
         pltpu.make_async_copy(left_ref, lraw, load_sem.at[0]),
         pltpu.make_async_copy(right_ref, rraw, load_sem.at[1]),
     ]
+    small = [
+        pltpu.make_async_copy(dims_hbm, dims_ref, load_sem.at[4]),
+        pltpu.make_async_copy(links_hbm, links_ref, load_sem.at[5]),
+    ]
     trial_load.start()
+    for load in small:
+        load.start()
     for load in loads:
         load.start()
     pre_load.start()
 
-    if sectors == 4:
-        to_sector = [
-            me_s + 1 - 2 * lax.rem(me_s, 2),
-            lax.rem(me_s + 2, 4),
-            3 - me_s,
-        ]
-        from_sector = to_sector
-    else:
-        to_sector = [ring(me_s, d, sectors) for d in range(1, sectors)]
-        from_sector = [ring(me_s, -d, sectors) for d in range(1, sectors)]
-    sources = [me_s] + from_sector
-
-    def slab(ag, s, t):
-        return gath.at[ag, pl.ds(pl.multiple_of(s * width + t * rows, rows), rows)]
-
-    def slab_copy(ag, s, t, to_s, to_t, k):
-        here = slab(ag, s, t)
+    def slab(ag, s, t, p):
+        at = s * width + t * rows + p * piece
+        return gath.at[ag, pl.ds(pl.multiple_of(at, piece), piece)]
+
+    def slab_copy(ag, s, t, p, to_s, to_t, k):
+        here = slab(ag, s, t, p)
         return pltpu.make_async_remote_copy(
             src_ref=here, dst_ref=here,
-            send_sem=ag_send.at[ag, k], recv_sem=ag_recv.at[ag, s * terms + t],
+            send_sem=ag_send.at[ag, k], recv_sem=ag_recv.at[ag, (s * terms + t) * parts + p],
             device_id={"term": to_t, "sector": to_s}, device_id_type=MESH,
         )
 
-    def arrive(ag, s, t):
-        slab_copy(ag, s, t, ring(me_s, 1, sectors), me_t, 0).wait_recv()
-
-    k_x = sectors - 1
-    k_c = k_x + (chips - 1) * sectors
-    n_send = k_c + chips * sectors
-
-    def to_chips(ag, s, d):
-        for e in range(1, chips):
+    def arrive(ag, s, t, p):
+        slab_copy(ag, s, t, p, ring(me_s, 1, sectors), me_t, 0).wait_recv()
+
+    n_send = (sectors * terms - 1) * parts
+
+    if quad:
+        near_s = [me_s, me_s + 1 - 2 * lax.rem(me_s, 2), lax.rem(me_s + 2, 4), 3 - me_s]
+        near_x = [me_x, 1 - me_x]
+        near_c = [me_c, other_c]
+
+        def place(rel):
+            return near_s[rel[0]], term_at(near_x[rel[1]], near_c[rel[2]])
+
+        here, core, chip, near, diag = (0, 0, 0), (0, 0, 1), (0, 1, 0), (1, 0, 0), (1, 1, 0)
+        across, far = (2, 0, 0), (3, 1, 0)
+        after = [chip, near, diag, (2, 1, 0), (3, 0, 0), far]
+        begin_plan = [(here, to) for to in (across, chip, near, diag, far)] + [(here, core)]
+        relay_plan = [(across, to) for to in (chip, near)] + [(across, core)]
+        sends = [(a, to, p) for a, to in begin_plan + relay_plan for p in range(parts)]
+        sends += [(a, core, p) for a in after for p in range(parts)]
+        index = {send: k for k, send in enumerate(sends)}
+
+        def push(ag, a, to, p):
+            slab_copy(ag, *place(a), p, *place(to), index[a, to, p]).start()
+
+        def gather_start(ag):
+            for a, to in begin_plan:
+                for p in range(parts):
+                    push(ag, a, to, p)
+
+        def gather_relay(ag):
+            for p in range(parts):
+                arrive(ag, *place(across), p)
+                for a, to in relay_plan:
+                    push(ag, a, to, p)
+
+        def gather_finish(ag):
+            for a in after:
+                for p in range(parts):
+                    arrive(ag, *place(a), p)
+                    push(ag, a, core, p)
+            for a in [here, across] + after:
+                for p in range(parts):
+                    arrive(ag, *place((a[0], a[1], 1)), p)
+    else:
+        k_x = sectors - 1
+        k_c = k_x + (chips - 1) * sectors
+
+        def to_chips(ag, s, d):
+            for e in range(1, chips):
+                slab_copy(
+                    ag, s, me_t, 0, me_s, term_at(ring(me_x, e, chips), me_c),
+                    k_x + (e - 1) * sectors + d,
+                ).start()
+
+        def to_core(ag, s, x, d, e):
             slab_copy(
-                ag, s, me_t, me_s, term_at(ring(me_x, e, chips), me_c),
-                k_x + (e - 1) * sectors + d,
+                ag, s, term_at(x, me_c), 0, me_s, term_at(me_x, other_c),
+                k_c + e * sectors + d,
             ).start()
 
-    def to_core(ag, s, x, d, e):
-        slab_copy(
-            ag, s, term_at(x, me_c), me_s, term_at(me_x, other_c), k_c + e * sectors + d
-        ).start()
-
-    def gather_start(ag):
-        for d in range(1, sectors):
-            slab_copy(ag, me_s, me_t, to_sector[d - 1], me_t, d - 1).start()
-        to_chips(ag, me_s, 0)
-        to_core(ag, me_s, me_x, 0, 0)
-
-    def gather_sector(ag):
-        for d in range(1, sectors):
-            s = sources[d]
-            arrive(ag, s, me_t)
-            to_chips(ag, s, d)
-            to_core(ag, s, me_x, d, 0)
-
-    def gather_chip(ag):
-        for e in range(1, chips):
-            x = ring(me_x, -e, chips)
-            for d in range(sectors):
-                s = sources[d]
-                arrive(ag, s, term_at(x, me_c))
-                to_core(ag, s, x, d, e)
-
-    def gather_core(ag):
-        for e in range(chips):
-            x = ring(me_x, -e, chips)
-            for d in range(sectors):
-                arrive(ag, sources[d], term_at(x, other_c))
-
-    def gather_rest(ag):
-        gather_sector(ag)
-        gather_chip(ag)
-        gather_core(ag)
+        def gather_start(ag):
+            for d in range(1, sectors):
+                slab_copy(ag, me_s, me_t, 0, ring(me_s, d, sectors), me_t, d - 1).start()
+            to_chips(ag, me_s, 0)
+            to_core(ag, me_s, me_x, 0, 0)
+
+        def gather_relay(ag):
+            for d in range(1, sectors):
+                s = ring(me_s, -d, sectors)
+                arrive(ag, s, me_t, 0)
+                to_chips(ag, s, d)
+                to_core(ag, s, me_x, d, 0)
+
+        def gather_finish(ag):
+            for e in range(1, chips):
+                x = ring(me_x, -e, chips)
+                for d in range(sectors):
+                    s = ring(me_s, -d, sectors)
+                    arrive(ag, s, term_at(x, me_c), 0)
+                    to_core(ag, s, x, d, e)
+            for e in range(chips):
+                x = ring(me_x, -e, chips)
+                for d in range(sectors):
+                    arrive(ag, ring(me_s, -d, sectors), term_at(x, other_c), 0)
 
     def fold(value):
         return jnp.sum(value.reshape(CHUNK // 8, 8, width), axis=0)
@@ -177,6 +211,8 @@
 
         lax.fori_loop(0, steps, step, 0, unroll=2)
 
+    for load in small:
+        load.wait()
     row_index = me_t * rows + lax.broadcasted_iota(jnp.int32, (rows, width), 0)
     col_index = lax.broadcasted_iota(jnp.int32, (rows, width), 1)
     live = (row_index < dims_ref[0]) & (col_index < dims_ref[1])
@@ -201,10 +237,9 @@
         rcat[pl.ds(base + 2 * width, width), :] = high
         return carry
 
-    gather_sector(first)
+    gather_relay(first)
     lax.fori_loop(0, own_terms, prepare, 0)
-    gather_chip(first)
-    gather_core(first)
+    gather_finish(first)
     pre_load.wait()
     gather_start(pre)
 
@@ -250,16 +285,16 @@
 
     multiply(0)
     rs_start(0)
-    gather_sector(pre)
+    gather_relay(pre)
     collect(0)
-    gather_chip(pre)
-    gather_core(pre)
+    gather_finish(pre)
 
     def invert(i, at):
         pinv[at, :] = 1.0 / gath[pre, at, :]
 
     over_chunks(invert)
-    gather_rest(0)
+    gather_relay(0)
+    gather_finish(0)
     (theta,) = dots(lambda at: (vec[at, :] * gath[0, at, :],), 1)
 
     def begin_residual(i, at):
@@ -295,7 +330,8 @@
         rs_start(it)
         known = dots(early, 5)
         collect(it)
-        gather_rest(it)
+        gather_relay(it)
+        gather_finish(it)
 
         def late(at):
             h = gath[it, at, :]
@@ -360,7 +396,7 @@
 
     def finish(ag, carry):
         for k in range(n_send):
-            slab_copy(ag, me_s, me_t, ring(me_s, 1, sectors), me_t, k).wait_send()
+            slab_copy(ag, me_s, me_t, 0, ring(me_s, 1, sectors), me_t, k).wait_send()
         return carry
 
     lax.fori_loop(0, ITERS + 2, finish, 0)
@@ -385,7 +421,6 @@
     gathers = ITERS + 2
     whole = (sectors * width, width)
     vmem = pl.BlockSpec(memory_space=pltpu.VMEM)
-    smem = pl.BlockSpec(memory_space=pltpu.SMEM)
     hbm = pl.BlockSpec(memory_space=pltpu.HBM)
     ground, energy = pl.pallas_call(
         functools.partial(kernel, sectors, terms, count),
@@ -393,7 +428,7 @@
             jax.ShapeDtypeStruct((rows, width), F32),
             jax.ShapeDtypeStruct((1, 128), F32),
         ),
-        in_specs=[smem, smem, hbm, hbm, hbm, hbm],
+        in_specs=[hbm] * 6,
         out_specs=(vmem, vmem),
         scratch_shapes=[
             pltpu.VMEM((gathers,) + whole, F32),
@@ -411,16 +446,18 @@
             pltpu.VMEM((own_terms, width, width), F32),
             pltpu.VMEM((rows, width), F32),
             pltpu.VMEM((sectors * terms, 16, width), F32),
-            pltpu.SemaphoreType.DMA((gathers, sectors * terms)),
-            pltpu.SemaphoreType.DMA((gathers, sectors * terms)),
+            pltpu.SMEM((own_terms,), jnp.int32),
+            pltpu.SMEM((2,), jnp.int32),
+            pltpu.SemaphoreType.DMA((gathers, sectors * terms * PARTS)),
+            pltpu.SemaphoreType.DMA((gathers, sectors * terms * PARTS)),
             pltpu.SemaphoreType.DMA((ITERS, terms - 1)),
             pltpu.SemaphoreType.DMA((ITERS, terms - 1)),
             pltpu.SemaphoreType.DMA((sectors * terms,)),
             pltpu.SemaphoreType.DMA((sectors * terms,)),
-            pltpu.SemaphoreType.DMA((4,)),
+            pltpu.SemaphoreType.DMA((6,)),
         ],
         compiler_params=pltpu.CompilerParams(
-            collective_id=0, has_side_effects=True, vmem_limit_bytes=52 * 2**20
+            collective_id=0, has_side_effects=True, vmem_limit_bytes=60 * 2**20
         ),
     )(
         links.reshape(own_terms),

time: 92.5 us -> 85.5 us (0.924)
  Pallas kernels: 85.4 us -> 80.9 us
  local copies, waits for them, and re-layouts: 5.02 us -> 1.47 us
    pallas_call x1, Pallas kernels: 85.4 us -> 80.9 us  [on_device(): pl.pallas_call(functools.partial(kernel, sectors, terms, count), out_shap...]
    unnamed x11 -> x1, local copies, waits for them, and re-layouts: 5.02 us -> 1.47 us
where the time goes in v3:
time: 85.5 us; the launch traced here: 84.7 us
  Pallas kernels  80.9 us (95%)
  between operations  2.39 us (3%)
  local copies, waits for them, and re-layouts  1.47 us (2%)
    pallas_call x1, Pallas kernels, on_device(): pl.pallas_call(functools.partial(kernel, sectors, terms, count), out_shap...  80.9 us

profile of v3, /device:TPU:0, one launch (start us, length us, event | category | flops | bytes accessed | tf_op | source)
XLA Modules:
  0.0 84.7 jit_solution(11647285010220297604)
XLA Ops:
  0.6 80.9 %shard_map.77 = (f32[64,256]{1,0:T(8,128)}, f32[1,128]{1,0:T(1,128)}) custom-call(s32[6]{0:T(128)} %bitcast.14, s32[2]{0:T(128)} %bitcast.15, f32[64,256]{1,0:T(8,128)} %bitcast.11, f32[64,256]{1,0:T(8,128)} %bitcast.12, f32[6,256,256]{2,1,0:T(8,128)} %bitcast.9, f32[6,256,256]{2,1,0:T(8,128)} %bitcast.10), custom_call_target="tpu_custom_call" | custom-call | tf_op jit(solution)/shard_map/pallas_call | solution.py:425
  81.5 1.5 %copy.10 = f32[1,64,256]{2,1,0:T(8,128)} copy(f32[1,64,256]{2,1,0:T(8,128)} %bitcast.13) | data formatting | bytes 131072

commit v4 on v3

--- a/solution.py
+++ b/solution.py
@@ -83,18 +83,26 @@
         at = s * width + t * rows + p * piece
         return gath.at[ag, pl.ds(pl.multiple_of(at, piece), piece)]
 
-    def slab_copy(ag, s, t, p, to_s, to_t, k):
+    def slab_copy(ag, s, t, p, to_s, to_t):
         here = slab(ag, s, t, p)
         return pltpu.make_async_remote_copy(
             src_ref=here, dst_ref=here,
-            send_sem=ag_send.at[ag, k], recv_sem=ag_recv.at[ag, (s * terms + t) * parts + p],
+            send_sem=ag_send.at[ag], recv_sem=ag_recv.at[ag, (s * terms + t) * parts + p],
             device_id={"term": to_t, "sector": to_s}, device_id_type=MESH,
         )
 
     def arrive(ag, s, t, p):
-        slab_copy(ag, s, t, p, ring(me_s, 1, sectors), me_t, 0).wait_recv()
-
-    n_send = (sectors * terms - 1) * parts
+        slab_copy(ag, s, t, p, ring(me_s, 1, sectors), me_t).wait_recv()
+
+    def sent(ref, sem):
+        pltpu.make_async_remote_copy(
+            src_ref=ref, dst_ref=ref, send_sem=sem, recv_sem=ag_recv.at[0, 0],
+            device_id={"sector": ring(me_s, 1, sectors)}, device_id_type=MESH,
+        ).wait_send()
+
+    def gather_sent(ag):
+        sent(gath.at[ag, pl.ds(0, (sectors * terms - 1) * rows)], ag_send.at[ag])
+
 
     if quad:
         near_s = [me_s, me_s + 1 - 2 * lax.rem(me_s, 2), lax.rem(me_s + 2, 4), 3 - me_s]
@@ -109,12 +117,9 @@
         after = [chip, near, diag, (2, 1, 0), (3, 0, 0), far]
         begin_plan = [(here, to) for to in (across, chip, near, diag, far)] + [(here, core)]
         relay_plan = [(across, to) for to in (chip, near)] + [(across, core)]
-        sends = [(a, to, p) for a, to in begin_plan + relay_plan for p in range(parts)]
-        sends += [(a, core, p) for a in after for p in range(parts)]
-        index = {send: k for k, send in enumerate(sends)}
 
         def push(ag, a, to, p):
-            slab_copy(ag, *place(a), p, *place(to), index[a, to, p]).start()
+            slab_copy(ag, *place(a), p, *place(to)).start()
 
         def gather_start(ag):
             for a, to in begin_plan:
@@ -136,34 +141,29 @@
                 for p in range(parts):
                     arrive(ag, *place((a[0], a[1], 1)), p)
     else:
-        k_x = sectors - 1
-        k_c = k_x + (chips - 1) * sectors
-
-        def to_chips(ag, s, d):
+        def to_chips(ag, s):
             for e in range(1, chips):
                 slab_copy(
-                    ag, s, me_t, 0, me_s, term_at(ring(me_x, e, chips), me_c),
-                    k_x + (e - 1) * sectors + d,
+                    ag, s, me_t, 0, me_s, term_at(ring(me_x, e, chips), me_c)
                 ).start()
 
-        def to_core(ag, s, x, d, e):
+        def to_core(ag, s, x):
             slab_copy(
-                ag, s, term_at(x, me_c), 0, me_s, term_at(me_x, other_c),
-                k_c + e * sectors + d,
+                ag, s, term_at(x, me_c), 0, me_s, term_at(me_x, other_c)
             ).start()
 
         def gather_start(ag):
             for d in range(1, sectors):
-                slab_copy(ag, me_s, me_t, 0, ring(me_s, d, sectors), me_t, d - 1).start()
-            to_chips(ag, me_s, 0)
-            to_core(ag, me_s, me_x, 0, 0)
+                slab_copy(ag, me_s, me_t, 0, ring(me_s, d, sectors), me_t).start()
+            to_chips(ag, me_s)
+            to_core(ag, me_s, me_x)
 
         def gather_relay(ag):
             for d in range(1, sectors):
                 s = ring(me_s, -d, sectors)
                 arrive(ag, s, me_t, 0)
-                to_chips(ag, s, d)
-                to_core(ag, s, me_x, d, 0)
+                to_chips(ag, s)
+                to_core(ag, s, me_x)
 
         def gather_finish(ag):
             for e in range(1, chips):
@@ -171,7 +171,7 @@
                 for d in range(sectors):
                     s = ring(me_s, -d, sectors)
                     arrive(ag, s, term_at(x, me_c), 0)
-                    to_core(ag, s, x, d, e)
+                    to_core(ag, s, x)
             for e in range(chips):
                 x = ring(me_x, -e, chips)
                 for d in range(sectors):
@@ -242,6 +242,7 @@
     gather_finish(first)
     pre_load.wait()
     gather_start(pre)
+    gather_sent(first)
 
     (norm,) = dots(lambda at: (gath[first, at, :] * gath[first, at, :],), 1)
     scale = 1.0 / jnp.sqrt(norm + EPS)
@@ -253,8 +254,13 @@
 
     over_chunks(begin)
 
+    if quad:
+        rows_to = [term_at(1 - me_x, me_c), term_at(1 - me_x, other_c), term_at(me_x, other_c)]
+    else:
+        rows_to = [ring(me_t, d, terms) for d in range(1, terms)]
+
     def rs_copy(it, d):
-        to = ring(me_t, d, terms)
+        to = rows_to[d - 1]
         return pltpu.make_async_remote_copy(
             src_ref=part.at[it, pl.ds(pl.multiple_of(to * rows, rows), rows)],
             dst_ref=rsbuf.at[it, d - 1],
@@ -262,18 +268,24 @@
             device_id={"term": to}, device_id_type=MESH,
         )
 
-    def multiply(it):
+    def multiply(it, last=False):
         for k in range(own_terms):
             inner = jnp.dot(lcat[k], xcat[links_ref[k]], preferred_element_type=F32)
             high, low = split(inner)
             icat[:, k * wide : k * wide + width] = high
             icat[:, k * wide + width : k * wide + 2 * width] = high
             icat[:, k * wide + 2 * width : (k + 1) * wide] = low
+        if quad and not last:
+            for x, sends in ((1 - me_x, (1, 2)), (me_x, (3,))):
+                at = pl.ds(pl.multiple_of(x * (width // 2), width // 2), width // 2)
+                part[it, at, :] = jnp.dot(icat[at, :], rcat[...], preferred_element_type=F32)
+                for d in sends:
+                    rs_copy(it, d).start()
+            return
         part[it] = jnp.dot(icat[...], rcat[...], preferred_element_type=F32)
-
-    def rs_start(it):
-        for d in range(1, terms):
-            rs_copy(it, d).start()
+        if not last:
+            for d in range(1, terms):
+                rs_copy(it, d).start()
 
     def collect(it):
         total = part[it, pl.ds(pl.multiple_of(me_t * rows, rows), rows), :]
@@ -284,7 +296,6 @@
         gather_start(it)
 
     multiply(0)
-    rs_start(0)
     gather_relay(pre)
     collect(0)
     gather_finish(pre)
@@ -327,8 +338,8 @@
 
     def iterate(it, theta):
         multiply(it)
-        rs_start(it)
         known = dots(early, 5)
+        gather_sent(it - 1)
         collect(it)
         gather_relay(it)
         gather_finish(it)
@@ -354,14 +365,14 @@
 
     theta = lax.fori_loop(1, ITERS, iterate, theta)
 
-    multiply(ITERS)
+    multiply(ITERS, last=True)
     me = me_s * terms + me_t
 
     def sc_copy(k):
         a, b = others[k]
         return pltpu.make_async_remote_copy(
             src_ref=scal.at[me], dst_ref=scal.at[me],
-            send_sem=sc_send.at[k], recv_sem=sc_recv.at[me],
+            send_sem=sc_send.at[0], recv_sem=sc_recv.at[me],
             device_id={"term": ring(me_t, b, terms), "sector": ring(me_s, a, sectors)},
             device_id_type=MESH,
         )
@@ -372,11 +383,20 @@
         h = part[ITERS, i * CHUNK : (i + 1) * CHUNK, :]
         vh = vh + fold(vec[at, :] * h)
         rh = rh + fold(res[at, :] * h)
-    scal[me, 0:8, :] = vh
-    scal[me, 8:16, :] = rh
+    def narrow(value):
+        value = value[0:4] + value[4:8]
+        return sum(value[:, i * 128 : (i + 1) * 128] for i in range(width // 128))
+
+    scal[me, 0:4, :] = narrow(vh)
+    scal[me, 4:8, :] = narrow(rh)
     for k in range(len(others)):
         sc_copy(k).start()
     known = dots(early, 5)
+    gather_sent(pre)
+    gather_sent(ITERS - 1)
+    for it in range(ITERS):
+        for d in range(1, terms):
+            rs_copy(it, d).wait_send()
     for a, b in others:
         source = ring(me_s, a, sectors) * terms + ring(me_t, b, terms)
         pltpu.make_async_remote_copy(
@@ -390,25 +410,11 @@
         value = jnp.sum(value, axis=0, keepdims=True)
         return jnp.sum(value, axis=1, keepdims=True) / count
 
-    theta, c_old, c_new = rotate(theta, *known, whole_sum(sums[0:8]), whole_sum(sums[8:16]))
+    theta, c_old, c_new = rotate(theta, *known, whole_sum(sums[0:4]), whole_sum(sums[4:8]))
     ground_ref[...] = c_old * vec[own, :] + c_new * res[own, :]
     energy_ref[...] = jnp.broadcast_to(theta, energy_ref.shape)
 
-    def finish(ag, carry):
-        for k in range(n_send):
-            slab_copy(ag, me_s, me_t, 0, ring(me_s, 1, sectors), me_t, k).wait_send()
-        return carry
-
-    lax.fori_loop(0, ITERS + 2, finish, 0)
-
-    def finish_rs(it, carry):
-        for d in range(1, terms):
-            rs_copy(it, d).wait_send()
-        return carry
-
-    lax.fori_loop(0, ITERS, finish_rs, 0)
-    for k in range(len(others)):
-        sc_copy(k).wait_send()
+    sent(scal.at[pl.ds(0, len(others))], sc_send.at[0])
 
 
 def on_device(trial, precond, left_ops, right_ops, links, block_dims):
@@ -445,14 +451,14 @@
             pltpu.VMEM((own_terms, width, width), F32),
             pltpu.VMEM((own_terms, width, width), F32),
             pltpu.VMEM((rows, width), F32),
-            pltpu.VMEM((sectors * terms, 16, width), F32),
+            pltpu.VMEM((sectors * terms, 8, 128), F32),
             pltpu.SMEM((own_terms,), jnp.int32),
             pltpu.SMEM((2,), jnp.int32),
-            pltpu.SemaphoreType.DMA((gathers, sectors * terms * PARTS)),
+            pltpu.SemaphoreType.DMA((gathers,)),
             pltpu.SemaphoreType.DMA((gathers, sectors * terms * PARTS)),
             pltpu.SemaphoreType.DMA((ITERS, terms - 1)),
             pltpu.SemaphoreType.DMA((ITERS, terms - 1)),
-            pltpu.SemaphoreType.DMA((sectors * terms,)),
+            pltpu.SemaphoreType.DMA((1,)),
             pltpu.SemaphoreType.DMA((sectors * terms,)),
             pltpu.SemaphoreType.DMA((6,)),
         ],

time: 85.5 us -> 83.3 us (0.974)
  Pallas kernels: 80.9 us -> 79.3 us
    pallas_call x1, Pallas kernels: 80.9 us -> 79.3 us  [on_device(): pl.pallas_call(functools.partial(kernel, sectors, terms, count), out_shap...]
where the time goes in v4:
time: 83.3 us; the launch traced here: 83.1 us
  Pallas kernels  79.3 us (95%)
  between operations  2.39 us (3%)
  local copies, waits for them, and re-layouts  1.47 us (2%)
    pallas_call x1, Pallas kernels, on_device(): pl.pallas_call(functools.partial(kernel, sectors, terms, count), out_shap...  79.3 us

profile of v4, /device:TPU:0, one launch (start us, length us, event | category | flops | bytes accessed | tf_op | source)
XLA Modules:
  0.0 83.1 jit_solution(15527423091168882124)
XLA Ops:
  0.6 79.3 %shard_map.77 = (f32[64,256]{1,0:T(8,128)}, f32[1,128]{1,0:T(1,128)}) custom-call(s32[6]{0:T(128)} %bitcast.14, s32[2]{0:T(128)} %bitcast.15, f32[64,256]{1,0:T(8,128)} %bitcast.11, f32[64,256]{1,0:T(8,128)} %bitcast.12, f32[6,256,256]{2,1,0:T(8,128)} %bitcast.9, f32[6,256,256]{2,1,0:T(8,128)} %bitcast.10), custom_call_target="tpu_custom_call" | custom-call | tf_op jit(solution)/shard_map/pallas_call | solution.py:431
  79.9 1.5 %copy.10 = f32[1,64,256]{2,1,0:T(8,128)} copy(f32[1,64,256]{2,1,0:T(8,128)} %bitcast.13) | data formatting | bytes 131072
